TPU v7x, 256 devices: a whole 4x4x8 slice. The times are simulated.
256 devices in a mesh: section: 8 (over z), uly: 32 (over x, y, core).
Axes of the slice: x: 4, y: 4, z: 8, core: 2. Of those that a mesh axis runs over, the one named last changes fastest.
Arguments:
- query: bfloat16 [8, 1536, 4096], P('section', 'uly')
- fresh_keys: bfloat16 [8, 1536, 4096], P('section', 'uly'), may hold values from -6 to 6
- fresh_values: bfloat16 [8, 1536, 4096], P('section', 'uly'), may hold values from -6 to 6
- stale_keys: bfloat16 [8, 12288, 4096], P('section', None, 'uly')
- stale_values: bfloat16 [8, 12288, 4096], P('section', None, 'uly'), may hold values from -6 to 6
- next_gain: float32 [8, 4096], P('section'), may hold values from 0.1 to 1.9
- patch_index: int32 [8], P('section'), may hold values from 0 to 7, as said below
Outputs:
- handoff: bfloat16 [8, 1536, 4096], P('section', 'uly')
Inputs may be any that keep to these rules, and one draw needn't show every extreme that they name: patch_index[s] = (t - s) mod 8 for one tick t of 0 to 6.
All inputs are finite; a program needn't handle non-finite values.
Results may differ from a plain program's by a relative error of at most 0.01.
Values may be sent and summed in bfloat16 or wider, within the bound.
A program may use at most 64 MiB of HBM per device.

v0:
```python
import functools
import math

import jax
import jax.numpy as jnp
from jax import lax
from jax.experimental import pallas as pl
from jax.experimental.pallas import tpu as pltpu
from jax.sharding import PartitionSpec as P

MESH = pl.DeviceIdType.MESH
NT = (((1,), (1,)), ((), ()))
SIDE = 4

FIRST = ((0, 0), (0, 1), (0, 3), (1, 0))
MIDDLE = ((3, 0), (0, 2), (2, 0), (1, 2), (3, 2), (2, 1), (2, 3), (2, 2))
LAST = ((1, 1), (3, 3), (1, 3), (3, 1))
GROUPS = tuple(
    tuple((dx, dy, dc) for dx, dy in chips for dc in (0, 1)) for chips in (FIRST, MIDDLE, LAST)
)
SLOTS = sum(GROUPS, ())


def lane_max(scores):
    width = 128
    highest = scores[:, :width]
    for start in range(width, scores.shape[1], width):
        highest = jnp.maximum(highest, scores[:, start : start + width])
    return jnp.max(highest, axis=1, keepdims=True)


def kernel(
    scale,
    patch_ref,
    query_ref,
    fresh_k_ref,
    fresh_v_ref,
    stale_k_ref,
    stale_v_ref,
    gain_ref,
    out_ref,
    keys,
    values,
    q_all,
    new_k,
    new_v,
    done,
    arrived,
    s0,
    s1,
    m0,
    m1,
    weighted,
    total,
    running,
    load_sem,
    q_sem,
    kv_sem,
    send_sem,
    out_send_sem,
    out_recv_sem,
    ready_sem,
):
    section = lax.axis_index("section")
    me = lax.axis_index("uly")
    sections = lax.axis_size("section")
    after = lax.rem(section + 1, sections)
    before = lax.rem(section + sections - 1, sections)
    x, y, core = me // (2 * SIDE), lax.rem(me // 2, SIDE), lax.rem(me, 2)
    rows, head = query_ref.shape[0], keys.shape[1]
    patch = q_all.shape[0]
    patches = keys.shape[0] // patch

    def device(dx, dy, dc):
        other = core if dc == 0 else 1 - core
        return (lax.rem(x + dx, SIDE) * SIDE + lax.rem(y + dy, SIDE)) * 2 + other

    def owner(slot):
        return device(*slot)

    def holder(slot):
        dx, dy, dc = slot
        return device((SIDE - dx) % SIDE, (SIDE - dy) % SIDE, dc)

    def columns(device_index):
        return pl.ds(pl.multiple_of(device_index * head, head), head)

    load_k = pltpu.make_async_copy(stale_k_ref, keys, load_sem.at[0])
    load_v = pltpu.make_async_copy(stale_v_ref, values, load_sem.at[1])
    load_k.start()
    load_v.start()

    barrier = pltpu.get_barrier_semaphore()
    for slot in SLOTS[1:]:
        pl.semaphore_signal(barrier, inc=1, device_id=(section, owner(slot)), device_id_type=MESH)
    pl.semaphore_signal(barrier, inc=1, device_id=(after, me), device_id_type=MESH)
    pl.semaphore_wait(barrier, len(SLOTS))
    pl.semaphore_signal(ready_sem, inc=1, device_id=(before, me), device_id_type=MESH)

    def send(source, k, target, send_to, receive_to):
        slot = SLOTS[k]
        if k == 0:
            pltpu.make_async_copy(
                source.at[:, columns(me)], target.at[pl.ds(0, rows), :], receive_to
            ).start()
            return
        there = holder(slot)
        pltpu.make_async_remote_copy(
            src_ref=source.at[:, columns(there)],
            dst_ref=target.at[pl.ds(k * rows, rows), :],
            send_sem=send_to,
            recv_sem=receive_to,
            device_id=(section, there),
            device_id_type=MESH,
        ).start()

    bounds, first = [], 0
    for g, group in enumerate(GROUPS):
        for k in range(first, first + len(group)):
            send(query_ref, k, q_all, send_sem.at[0], q_sem.at[g])
        bounds.append((first, first + len(group)))
        first += len(group)
    for k in range(len(SLOTS)):
        send(fresh_k_ref, k, new_k, send_sem.at[1], kv_sem.at[0])
        send(fresh_v_ref, k, new_v, send_sem.at[2], kv_sem.at[1])

    def await_bytes(ref, sem):
        pltpu.make_async_copy(ref, ref, sem).wait()

    weighted[...] = jnp.zeros_like(weighted)
    total[...] = jnp.zeros_like(total)
    scores_of, highest_of = (s0, s1), (m0, m1)
    own_patch = patch_ref[0]

    def stale_block(ref, j):
        here = ref[pl.ds(pl.multiple_of(j * patch, patch), patch), :]
        later = ref[pl.ds(pl.multiple_of((j + 1) * patch, patch), patch), :]
        return jnp.where(own_patch > j, here, later)

    def score(low, high, j, b):
        n = high - low
        block = new_k[...] if j is None else stale_block(keys, j)
        s = lax.dot_general(q_all[low:high, :], block, NT, preferred_element_type=jnp.float32)
        scores_of[b][:n, :] = s
        highest_of[b][:n, :] = jnp.broadcast_to(lane_max(s), (n, 128))

    def weigh(low, high, j, b):
        n = high - low
        old = running[:n, :]
        new = jnp.maximum(old, highest_of[b][:n, :])
        running[:n, :] = new
        faded = jnp.exp2((old - new) * scale)
        wide = jnp.concatenate([new] * (patch // 128), axis=1)
        w = jnp.exp2((scores_of[b][:n, :] - wide) * scale).astype(jnp.bfloat16)
        block = new_v[...] if j is None else stale_block(values, j)
        block = jnp.concatenate([block, jnp.ones_like(block)], axis=1)
        product = jnp.dot(w, block, preferred_element_type=jnp.float32)
        weighted[:n, :] = weighted[:n, :] * faded + product[:, :head]
        total[:n, :] = total[:n, :] * faded + product[:, head:]

    load_k.wait()
    for g, (low_slot, high_slot) in enumerate(bounds):
        low, high = low_slot * rows, high_slot * rows
        running[...] = jnp.full_like(running, -jnp.inf)
        if g == 0:
            await_bytes(q_all.at[pl.ds(low, high - low), :], q_sem.at[g])
            score(low, high, 0, 0)
            load_v.wait()

        def two_blocks(u, carry, low=low, high=high):
            score(low, high, 2 * u + 1, 1)
            weigh(low, high, 2 * u, 0)
            score(low, high, 2 * u + 2, 0)
            weigh(low, high, 2 * u + 1, 1)
            return carry

        lax.fori_loop(0, (patches - 2) // 2, two_blocks, 0)
        if g == 0:
            await_bytes(new_k, kv_sem.at[0])
            await_bytes(new_v, kv_sem.at[1])
        if g + 1 < len(bounds):
            next_low, next_high = (slot * rows for slot in bounds[g + 1])
            await_bytes(q_all.at[pl.ds(next_low, next_high - next_low), :], q_sem.at[g + 1])
        score(low, high, None, 1)
        weigh(low, high, patches - 2, 0)
        if g + 1 < len(bounds):
            score(next_low, next_high, 0, 0)
        weigh(low, high, None, 1)
        n = high - low
        done[low:high, :] = (weighted[:n, :] / total[:n, :]).astype(jnp.bfloat16)
        if g == 0:
            pl.semaphore_wait(ready_sem, 1)
        for k in range(low_slot, high_slot):
            pltpu.make_async_remote_copy(
                src_ref=done.at[pl.ds(k * rows, rows), :],
                dst_ref=arrived.at[:, columns(me)],
                send_sem=out_send_sem,
                recv_sem=out_recv_sem,
                device_id=(after, owner(SLOTS[k])),
                device_id_type=MESH,
            ).start()

    for i, ref in enumerate((q_all, new_k, new_v)):
        await_bytes(ref.at[pl.ds(rows, patch - rows), :], send_sem.at[i])
    await_bytes(arrived, out_recv_sem)
    rows_in = arrived[...].astype(jnp.float32)
    mean_square = jnp.mean(rows_in * rows_in, axis=1, keepdims=True)
    out_ref[...] = (rows_in * lax.rsqrt(mean_square + 1e-06) * gain_ref[...]).astype(jnp.bfloat16)
    await_bytes(done, out_send_sem)


def shards(query, fresh_keys, fresh_values, stale_keys, stale_values, next_gain, patch_index):
    rows, width = query.shape[1:]
    length, head = stale_keys.shape[1:]
    devices = lax.axis_size("uly")
    patch = rows * devices
    scale = head ** (-0.5) / math.log(2.0)
    tallest = max(len(group) for group in GROUPS) * rows
    hbm = pl.BlockSpec(memory_space=pl.ANY)
    vmem = pl.BlockSpec(memory_space=pltpu.VMEM)
    bf16, f32 = jnp.bfloat16, jnp.float32
    out = pl.pallas_call(
        functools.partial(kernel, scale),
        out_shape=jax.ShapeDtypeStruct((rows, width), bf16),
        in_specs=[pl.BlockSpec(memory_space=pltpu.SMEM)] + [hbm] * 5 + [vmem],
        out_specs=vmem,
        scratch_shapes=[
            pltpu.VMEM((length, head), bf16),
            pltpu.VMEM((length, head), bf16),
            pltpu.VMEM((patch, head), bf16),
            pltpu.VMEM((patch, head), bf16),
            pltpu.VMEM((patch, head), bf16),
            pltpu.VMEM((patch, head), bf16),
            pltpu.VMEM((rows, width), bf16),
            pltpu.VMEM((tallest, patch), f32),
            pltpu.VMEM((tallest, patch), f32),
            pltpu.VMEM((tallest, 128), f32),
            pltpu.VMEM((tallest, 128), f32),
            pltpu.VMEM((tallest, head), f32),
            pltpu.VMEM((tallest, head), f32),
            pltpu.VMEM((tallest, 128), f32),
            pltpu.SemaphoreType.DMA((2,)),
            pltpu.SemaphoreType.DMA((len(GROUPS),)),
            pltpu.SemaphoreType.DMA((2,)),
            pltpu.SemaphoreType.DMA((3,)),
            pltpu.SemaphoreType.DMA,
            pltpu.SemaphoreType.DMA,
            pltpu.SemaphoreType.REGULAR,
        ],
        compiler_params=pltpu.CompilerParams(
            collective_id=0, has_side_effects=True, vmem_limit_bytes=56 << 20
        ),
        cost_estimate=pl.CostEstimate(
            flops=4 * patch * length * head,
            bytes_accessed=4 * length * head + 8 * rows * width,
            transcendentals=patch * length,
        ),
    )(patch_index, query[0], fresh_keys[0], fresh_values[0], stale_keys[0], stale_values[0], next_gain)
    return out[None]


def solution(mesh):
    in_specs = (
        P("section", "uly", None),
        P("section", "uly", None),
        P("section", "uly", None),
        P("section", None, "uly"),
        P("section", None, "uly"),
        P("section", None),
        P("section"),
    )
    out_specs = P("section", "uly", None)
    return jax.shard_map(shards, mesh=mesh, in_specs=in_specs, out_specs=out_specs, check_vma=False)
```

profile of v0, /device:TPU:1, one launch (start us, length us, event | category | flops | bytes accessed | tf_op | source)
XLA Modules:
  0.0 55.9 jit_solution(14113433828094697847)
XLA Ops:
  0.7 53.5 %shard_map.73 = bf16[48,4096]{1,0:T(8,128)(2,1)} custom-call(s32[1]{0:T(128)S(6)} %copy.9.patch_ref, bf16[48,4096]{1,0:T(8,128)(2,1)} %bitcast.9, bf16[48,4096]{1,0:T(8,128)(2,1)} %bitcast.10, bf16[48,4096]{1,0:T(8,128)(2,1)} %bitcast.11, bf16[12288,128]{1,0:T(8,128)(2,1)} %bitcast.7, bf16[12288,128]{1,0:T(8,128)(2,1)} %bitcast.8, f32[1,4096]{1,0:T(1,128)} %gain_ref.1), custom_call_target="tpu_custom_call" | custom-call | flops 9663676416 | bytes 7864320 | tf_op jit(solution)/shard_map/pallas_call | solution.py:222
  54.1 1.8 %copy.10 = bf16[1,48,4096]{2,1,0:T(8,128)(2,1)} copy(bf16[1,48,4096]{2,1,0:T(8,128)(2,1)} %bitcast.6) | data formatting | bytes 786432
where the time goes:
time: 56.1 us; the launch traced here: 55.9 us
  Pallas kernels  53.5 us (95%)
  local copies, waits for them, and re-layouts  1.77 us (3%)
  between operations  0.66 us (1%)
    pallas_call x1, Pallas kernels, shards(): pl.pallas_call(functools.partial(kernel, scale), out_shape=jax.ShapeDtype...  53.5 us
    unnamed x1, local copies, waits for them, and re-layouts  1.77 us

commit v1 on v0

--- a/solution.py
+++ b/solution.py
@@ -37,15 +37,13 @@
     fresh_v_ref,
     stale_k_ref,
     stale_v_ref,
-    gain_ref,
-    out_ref,
+    arrived,
     keys,
     values,
     q_all,
     new_k,
     new_v,
     done,
-    arrived,
     s0,
     s1,
     m0,
@@ -120,13 +118,11 @@
             send(query_ref, k, q_all, send_sem.at[0], q_sem.at[g])
         bounds.append((first, first + len(group)))
         first += len(group)
-    for k in range(len(SLOTS)):
-        send(fresh_k_ref, k, new_k, send_sem.at[1], kv_sem.at[0])
-        send(fresh_v_ref, k, new_v, send_sem.at[2], kv_sem.at[1])
 
     def await_bytes(ref, sem):
         pltpu.make_async_copy(ref, ref, sem).wait()
 
+    running[...] = jnp.full_like(running, -jnp.inf)
     weighted[...] = jnp.zeros_like(weighted)
     total[...] = jnp.zeros_like(total)
     scores_of, highest_of = (s0, s1), (m0, m1)
@@ -137,60 +133,49 @@
         later = ref[pl.ds(pl.multiple_of((j + 1) * patch, patch), patch), :]
         return jnp.where(own_patch > j, here, later)
 
-    def score(low, high, j, b):
+    def score(span, j, b):
+        low, high = span
         n = high - low
         block = new_k[...] if j is None else stale_block(keys, j)
         s = lax.dot_general(q_all[low:high, :], block, NT, preferred_element_type=jnp.float32)
         scores_of[b][:n, :] = s
         highest_of[b][:n, :] = jnp.broadcast_to(lane_max(s), (n, 128))
 
-    def weigh(low, high, j, b):
+    def weigh(span, j, b):
+        low, high = span
         n = high - low
-        old = running[:n, :]
+        old = running[low:high, :]
         new = jnp.maximum(old, highest_of[b][:n, :])
-        running[:n, :] = new
+        running[low:high, :] = new
         faded = jnp.exp2((old - new) * scale)
         wide = jnp.concatenate([new] * (patch // 128), axis=1)
         w = jnp.exp2((scores_of[b][:n, :] - wide) * scale).astype(jnp.bfloat16)
         block = new_v[...] if j is None else stale_block(values, j)
         block = jnp.concatenate([block, jnp.ones_like(block)], axis=1)
         product = jnp.dot(w, block, preferred_element_type=jnp.float32)
-        weighted[:n, :] = weighted[:n, :] * faded + product[:, :head]
-        total[:n, :] = total[:n, :] * faded + product[:, head:]
-
-    load_k.wait()
-    for g, (low_slot, high_slot) in enumerate(bounds):
-        low, high = low_slot * rows, high_slot * rows
-        running[...] = jnp.full_like(running, -jnp.inf)
-        if g == 0:
-            await_bytes(q_all.at[pl.ds(low, high - low), :], q_sem.at[g])
-            score(low, high, 0, 0)
-            load_v.wait()
-
-        def two_blocks(u, carry, low=low, high=high):
-            score(low, high, 2 * u + 1, 1)
-            weigh(low, high, 2 * u, 0)
-            score(low, high, 2 * u + 2, 0)
-            weigh(low, high, 2 * u + 1, 1)
+        weighted[low:high, :] = weighted[low:high, :] * faded + product[:, :head]
+        total[low:high, :] = total[low:high, :] * faded + product[:, head:]
+
+    spans = [(low * rows, high * rows) for low, high in bounds]
+
+    def await_queries(g):
+        low, high = spans[g]
+        await_bytes(q_all.at[pl.ds(low, high - low), :], q_sem.at[g])
+
+    def stale_blocks(span, b):
+        def two(u, carry):
+            score(span, 2 * u + 1, 1 - b)
+            weigh(span, 2 * u, b)
+            score(span, 2 * u + 2, b)
+            weigh(span, 2 * u + 1, 1 - b)
             return carry
 
-        lax.fori_loop(0, (patches - 2) // 2, two_blocks, 0)
-        if g == 0:
-            await_bytes(new_k, kv_sem.at[0])
-            await_bytes(new_v, kv_sem.at[1])
-        if g + 1 < len(bounds):
-            next_low, next_high = (slot * rows for slot in bounds[g + 1])
-            await_bytes(q_all.at[pl.ds(next_low, next_high - next_low), :], q_sem.at[g + 1])
-        score(low, high, None, 1)
-        weigh(low, high, patches - 2, 0)
-        if g + 1 < len(bounds):
-            score(next_low, next_high, 0, 0)
-        weigh(low, high, None, 1)
-        n = high - low
-        done[low:high, :] = (weighted[:n, :] / total[:n, :]).astype(jnp.bfloat16)
-        if g == 0:
-            pl.semaphore_wait(ready_sem, 1)
-        for k in range(low_slot, high_slot):
+        lax.fori_loop(0, (patches - 2) // 2, two, 0)
+
+    def hand_on(g):
+        low, high = spans[g]
+        done[low:high, :] = (weighted[low:high, :] / total[low:high, :]).astype(jnp.bfloat16)
+        for k in range(*bounds[g]):
             pltpu.make_async_remote_copy(
                 src_ref=done.at[pl.ds(k * rows, rows), :],
                 dst_ref=arrived.at[:, columns(me)],
@@ -200,13 +185,48 @@
                 device_id_type=MESH,
             ).start()
 
+    near, far, late = spans
+    final = patches - 2
+    load_k.wait()
+    await_queries(0)
+    score(near, 0, 0)
+    for k in range(len(SLOTS)):
+        send(fresh_k_ref, k, new_k, send_sem.at[1], kv_sem.at[0])
+        send(fresh_v_ref, k, new_v, send_sem.at[2], kv_sem.at[1])
+    load_v.wait()
+    stale_blocks(near, 0)
+    await_queries(1)
+    score(far, 0, 1)
+    weigh(near, final, 0)
+    stale_blocks(far, 1)
+    await_bytes(new_k, kv_sem.at[0])
+    score(near, None, 0)
+    weigh(far, final, 1)
+    await_bytes(new_v, kv_sem.at[1])
+    score(far, None, 1)
+    weigh(near, None, 0)
+    pl.semaphore_wait(ready_sem, 1)
+    hand_on(0)
+    await_queries(2)
+    score(late, 0, 0)
+    weigh(far, None, 1)
+    hand_on(1)
+    stale_blocks(late, 0)
+    score(late, None, 1)
+    weigh(late, final, 0)
+    weigh(late, None, 1)
+    hand_on(2)
+
     for i, ref in enumerate((q_all, new_k, new_v)):
         await_bytes(ref.at[pl.ds(rows, patch - rows), :], send_sem.at[i])
+    await_bytes(done, out_send_sem)
     await_bytes(arrived, out_recv_sem)
-    rows_in = arrived[...].astype(jnp.float32)
-    mean_square = jnp.mean(rows_in * rows_in, axis=1, keepdims=True)
-    out_ref[...] = (rows_in * lax.rsqrt(mean_square + 1e-06) * gain_ref[...]).astype(jnp.bfloat16)
-    await_bytes(done, out_send_sem)
+
+
+def norm_kernel(rows_ref, gain_ref, out_ref):
+    rows = rows_ref[...].astype(jnp.float32)
+    mean_square = jnp.mean(rows * rows, axis=1, keepdims=True)
+    out_ref[...] = (rows * lax.rsqrt(mean_square + 1e-06) * gain_ref[...]).astype(jnp.bfloat16)
 
 
 def shards(query, fresh_keys, fresh_values, stale_keys, stale_values, next_gain, patch_index):
@@ -217,13 +237,12 @@
     scale = head ** (-0.5) / math.log(2.0)
     tallest = max(len(group) for group in GROUPS) * rows
     hbm = pl.BlockSpec(memory_space=pl.ANY)
-    vmem = pl.BlockSpec(memory_space=pltpu.VMEM)
     bf16, f32 = jnp.bfloat16, jnp.float32
-    out = pl.pallas_call(
+    arriving = pl.pallas_call(
         functools.partial(kernel, scale),
         out_shape=jax.ShapeDtypeStruct((rows, width), bf16),
-        in_specs=[pl.BlockSpec(memory_space=pltpu.SMEM)] + [hbm] * 5 + [vmem],
-        out_specs=vmem,
+        in_specs=[pl.BlockSpec(memory_space=pltpu.SMEM)] + [hbm] * 5,
+        out_specs=hbm,
         scratch_shapes=[
             pltpu.VMEM((length, head), bf16),
             pltpu.VMEM((length, head), bf16),
@@ -231,14 +250,13 @@
             pltpu.VMEM((patch, head), bf16),
             pltpu.VMEM((patch, head), bf16),
             pltpu.VMEM((patch, head), bf16),
-            pltpu.VMEM((rows, width), bf16),
             pltpu.VMEM((tallest, patch), f32),
             pltpu.VMEM((tallest, patch), f32),
             pltpu.VMEM((tallest, 128), f32),
             pltpu.VMEM((tallest, 128), f32),
-            pltpu.VMEM((tallest, head), f32),
-            pltpu.VMEM((tallest, head), f32),
-            pltpu.VMEM((tallest, 128), f32),
+            pltpu.VMEM((patch, head), f32),
+            pltpu.VMEM((patch, head), f32),
+            pltpu.VMEM((patch, 128), f32),
             pltpu.SemaphoreType.DMA((2,)),
             pltpu.SemaphoreType.DMA((len(GROUPS),)),
             pltpu.SemaphoreType.DMA((2,)),
@@ -255,8 +273,11 @@
             bytes_accessed=4 * length * head + 8 * rows * width,
             transcendentals=patch * length,
         ),
-    )(patch_index, query[0], fresh_keys[0], fresh_values[0], stale_keys[0], stale_values[0], next_gain)
-    return out[None]
+    )(patch_index, query[0], fresh_keys[0], fresh_values[0], stale_keys[0], stale_values[0])
+    handoff = pl.pallas_call(norm_kernel, out_shape=jax.ShapeDtypeStruct((rows, width), bf16))(
+        arriving, next_gain
+    )
+    return handoff[None]
 
 
 def solution(mesh):

time: 56.1 us -> 49.6 us (0.88)
  Pallas kernels: 53.5 us -> 48.8 us
  local copies, waits for them, and re-layouts: 1.77 us -> 0 us
    pallas_call x1, Pallas kernels: 53.5 us -> 46.9 us  [shards(): pl.pallas_call(functools.partial(kernel, scale), out_shape=jax.ShapeDtype...]
    pallas_call x0 -> x1, Pallas kernels: none -> 1.94 us  [shards(): pl.pallas_call(norm_kernel, out_shape=jax.ShapeDtypeStruct((rows, width),...]
    unnamed x1 -> x0, local copies, waits for them, and re-layouts: 1.77 us -> none
where the time goes in v1:
time: 49.6 us; the launch traced here: 49.5 us
  Pallas kernels  48.8 us (98%)
  between operations  0.66 us (1%)
    pallas_call x1, Pallas kernels, shards(): pl.pallas_call(functools.partial(kernel, scale), out_shape=jax.ShapeDtype...  46.9 us
    pallas_call x1, Pallas kernels, shards(): pl.pallas_call(norm_kernel, out_shape=jax.ShapeDtypeStruct((rows, width),...  1.94 us

profile of v1, /device:TPU:1, one launch (start us, length us, event | category | flops | bytes accessed | tf_op | source)
XLA Modules:
  0.0 49.5 jit_solution(13520854966434839767)
XLA Ops:
  0.7 46.9 %shard_map.73.rows_ref = bf16[48,4096]{1,0:T(8,128)(2,1)} custom-call(s32[1]{0:T(128)S(6)} %copy.8.patch_ref, bf16[48,4096]{1,0:T(8,128)(2,1)} %bitcast.8, bf16[48,4096]{1,0:T(8,128)(2,1)} %bitcast.9, bf16[48,4096]{1,0:T(8,128)(2,1)} %bitcast.10, bf16[12288,128]{1,0:T(8,128)(2,1)} %bitcast.6, bf16[12288,128]{1,0:T(8,128)(2,1)} %bitcast.7), custom_call_target="tpu_custom_call" | custom-call | flops 9663676416 | bytes 7864320 | tf_op jit(solution)/shard_map/pallas_call | solution.py:241
  47.6 1.9 %shard_map.74 = bf16[48,4096]{1,0:T(8,128)(2,1)} custom-call(bf16[48,4096]{1,0:T(8,128)(2,1)} %shard_map.73.rows_ref, f32[1,4096]{1,0:T(1,128)} %gain_ref.1), custom_call_target="tpu_custom_call" | custom-call | tf_op jit(solution)/shard_map/pallas_call | solution.py:277

commit v2 on v1

--- a/solution.py
+++ b/solution.py
@@ -12,8 +12,8 @@
 NT = (((1,), (1,)), ((), ()))
 SIDE = 4
 
-FIRST = ((0, 0), (0, 1), (0, 3), (1, 0))
-MIDDLE = ((3, 0), (0, 2), (2, 0), (1, 2), (3, 2), (2, 1), (2, 3), (2, 2))
+FIRST = ((0, 0), (0, 1), (0, 3), (0, 2))
+MIDDLE = ((1, 0), (3, 0), (2, 0), (1, 2), (3, 2), (2, 1), (2, 3), (2, 2))
 LAST = ((1, 1), (3, 3), (1, 3), (3, 1))
 GROUPS = tuple(
     tuple((dx, dy, dc) for dx, dy in chips for dc in (0, 1)) for chips in (FIRST, MIDDLE, LAST)
@@ -57,6 +57,7 @@
     send_sem,
     out_send_sem,
     out_recv_sem,
+    row_sem,
     ready_sem,
 ):
     section = lax.axis_index("section")
@@ -89,11 +90,14 @@
     load_v.start()
 
     barrier = pltpu.get_barrier_semaphore()
-    for slot in SLOTS[1:]:
+    across = [(dx, 0, 0) for dx in range(1, SIDE)]
+    greeted = list(GROUPS[0][1:]) + across
+    for slot in greeted:
         pl.semaphore_signal(barrier, inc=1, device_id=(section, owner(slot)), device_id_type=MESH)
     pl.semaphore_signal(barrier, inc=1, device_id=(after, me), device_id_type=MESH)
-    pl.semaphore_wait(barrier, len(SLOTS))
-    pl.semaphore_signal(ready_sem, inc=1, device_id=(before, me), device_id_type=MESH)
+    pl.semaphore_wait(barrier, len(greeted) + 1)
+    for slot in across:
+        pl.semaphore_signal(row_sem, inc=1, device_id=(section, owner(slot)), device_id_type=MESH)
 
     def send(source, k, target, send_to, receive_to):
         slot = SLOTS[k]
@@ -114,6 +118,9 @@
 
     bounds, first = [], 0
     for g, group in enumerate(GROUPS):
+        if g == 1:
+            pl.semaphore_wait(row_sem, len(across))
+            pl.semaphore_signal(ready_sem, inc=1, device_id=(before, me), device_id_type=MESH)
         for k in range(first, first + len(group)):
             send(query_ref, k, q_all, send_sem.at[0], q_sem.at[g])
         bounds.append((first, first + len(group)))
@@ -264,6 +271,7 @@
             pltpu.SemaphoreType.DMA,
             pltpu.SemaphoreType.DMA,
             pltpu.SemaphoreType.REGULAR,
+            pltpu.SemaphoreType.REGULAR,
         ],
         compiler_params=pltpu.CompilerParams(
             collective_id=0, has_side_effects=True, vmem_limit_bytes=56 << 20

time: 49.6 us -> 47.5 us (0.958)
  Pallas kernels: 48.8 us -> 46.7 us
    pallas_call x1, Pallas kernels: 46.9 us -> 44.8 us  [shards(): pl.pallas_call(functools.partial(kernel, scale), out_shape=jax.ShapeDtype...]
where the time goes in v2:
time: 47.5 us; the launch traced here: 47.4 us
  Pallas kernels  46.7 us (98%)
  between operations  0.66 us (1%)
    pallas_call x1, Pallas kernels, shards(): pl.pallas_call(functools.partial(kernel, scale), out_shape=jax.ShapeDtype...  44.8 us
    pallas_call x1, Pallas kernels, shards(): pl.pallas_call(norm_kernel, out_shape=jax.ShapeDtypeStruct((rows, width),...  1.94 us

profile of v2, /device:TPU:1, one launch (start us, length us, event | category | flops | bytes accessed | tf_op | source)
XLA Modules:
  0.0 47.4 jit_solution(9777462776304289760)
XLA Ops:
  0.7 44.8 %shard_map.73.rows_ref = bf16[48,4096]{1,0:T(8,128)(2,1)} custom-call(s32[1]{0:T(128)S(6)} %copy.8.patch_ref, bf16[48,4096]{1,0:T(8,128)(2,1)} %bitcast.8, bf16[48,4096]{1,0:T(8,128)(2,1)} %bitcast.9, bf16[48,4096]{1,0:T(8,128)(2,1)} %bitcast.10, bf16[12288,128]{1,0:T(8,128)(2,1)} %bitcast.6, bf16[12288,128]{1,0:T(8,128)(2,1)} %bitcast.7), custom_call_target="tpu_custom_call" | custom-call | flops 9663676416 | bytes 7864320 | tf_op jit(solution)/shard_map/pallas_call | solution.py:248
  45.4 1.9 %shard_map.74 = bf16[48,4096]{1,0:T(8,128)(2,1)} custom-call(bf16[48,4096]{1,0:T(8,128)(2,1)} %shard_map.73.rows_ref, f32[1,4096]{1,0:T(1,128)} %gain_ref.1), custom_call_target="tpu_custom_call" | custom-call | tf_op jit(solution)/shard_map/pallas_call | solution.py:285

commit v3 on v2

--- a/solution.py
+++ b/solution.py
@@ -26,7 +26,7 @@
     highest = scores[:, :width]
     for start in range(width, scores.shape[1], width):
         highest = jnp.maximum(highest, scores[:, start : start + width])
-    return jnp.max(highest, axis=1, keepdims=True)
+    return highest
 
 
 def kernel(
@@ -146,17 +146,17 @@
         block = new_k[...] if j is None else stale_block(keys, j)
         s = lax.dot_general(q_all[low:high, :], block, NT, preferred_element_type=jnp.float32)
         scores_of[b][:n, :] = s
-        highest_of[b][:n, :] = jnp.broadcast_to(lane_max(s), (n, 128))
-
-    def weigh(span, j, b):
+        highest_of[b][:n, :] = lane_max(s)
+
+    def weigh(span, j, b, skip=0):
         low, high = span
-        n = high - low
+        stop = skip + high - low
         old = running[low:high, :]
-        new = jnp.maximum(old, highest_of[b][:n, :])
+        new = jnp.maximum(old, jnp.max(highest_of[b][skip:stop, :], axis=1, keepdims=True))
         running[low:high, :] = new
         faded = jnp.exp2((old - new) * scale)
         wide = jnp.concatenate([new] * (patch // 128), axis=1)
-        w = jnp.exp2((scores_of[b][:n, :] - wide) * scale).astype(jnp.bfloat16)
+        w = jnp.exp2((scores_of[b][skip:stop, :] - wide) * scale).astype(jnp.bfloat16)
         block = new_v[...] if j is None else stale_block(values, j)
         block = jnp.concatenate([block, jnp.ones_like(block)], axis=1)
         product = jnp.dot(w, block, preferred_element_type=jnp.float32)
@@ -179,10 +179,10 @@
 
         lax.fori_loop(0, (patches - 2) // 2, two, 0)
 
-    def hand_on(g):
-        low, high = spans[g]
+    def hand_on(slots):
+        low, high = slots[0] * rows, slots[1] * rows
         done[low:high, :] = (weighted[low:high, :] / total[low:high, :]).astype(jnp.bfloat16)
-        for k in range(*bounds[g]):
+        for k in range(*slots):
             pltpu.make_async_remote_copy(
                 src_ref=done.at[pl.ds(k * rows, rows), :],
                 dst_ref=arrived.at[:, columns(me)],
@@ -213,16 +213,19 @@
     score(far, None, 1)
     weigh(near, None, 0)
     pl.semaphore_wait(ready_sem, 1)
-    hand_on(0)
+    hand_on(bounds[0])
     await_queries(2)
     score(late, 0, 0)
     weigh(far, None, 1)
-    hand_on(1)
+    hand_on(bounds[1])
     stale_blocks(late, 0)
     score(late, None, 1)
     weigh(late, final, 0)
-    weigh(late, None, 1)
-    hand_on(2)
+    first, stop = bounds[2]
+    middle = (first + stop) // 2
+    for part in ((first, middle), (middle, stop)):
+        weigh((part[0] * rows, part[1] * rows), None, 1, (part[0] - first) * rows)
+        hand_on(part)
 
     for i, ref in enumerate((q_all, new_k, new_v)):
         await_bytes(ref.at[pl.ds(rows, patch - rows), :], send_sem.at[i])

time: 47.5 us -> 47.1 us (level)
  no operation moved by 1% of the time
where the time goes in v3:
time: 47.1 us; the launch traced here: 47 us
  Pallas kernels  46.3 us (98%)
  between operations  0.66 us (1%)
    pallas_call x1, Pallas kernels, shards(): pl.pallas_call(functools.partial(kernel, scale), out_shape=jax.ShapeDtype...  44.3 us
    pallas_call x1, Pallas kernels, shards(): pl.pallas_call(norm_kernel, out_shape=jax.ShapeDtypeStruct((rows, width),...  1.94 us

profile of v3, /device:TPU:1, one launch (start us, length us, event | category | flops | bytes accessed | tf_op | source)
XLA Modules:
  0.0 47.0 jit_solution(11044184424931360062)
XLA Ops:
  0.7 44.3 %shard_map.73.rows_ref = bf16[48,4096]{1,0:T(8,128)(2,1)} custom-call(s32[1]{0:T(128)S(6)} %copy.8.patch_ref, bf16[48,4096]{1,0:T(8,128)(2,1)} %bitcast.8, bf16[48,4096]{1,0:T(8,128)(2,1)} %bitcast.9, bf16[48,4096]{1,0:T(8,128)(2,1)} %bitcast.10, bf16[12288,128]{1,0:T(8,128)(2,1)} %bitcast.6, bf16[12288,128]{1,0:T(8,128)(2,1)} %bitcast.7), custom_call_target="tpu_custom_call" | custom-call | flops 9663676416 | bytes 7864320 | tf_op jit(solution)/shard_map/pallas_call | solution.py:251
  45.0 1.9 %shard_map.74 = bf16[48,4096]{1,0:T(8,128)(2,1)} custom-call(bf16[48,4096]{1,0:T(8,128)(2,1)} %shard_map.73.rows_ref, f32[1,4096]{1,0:T(1,128)} %gain_ref.1), custom_call_target="tpu_custom_call" | custom-call | tf_op jit(solution)/shard_map/pallas_call | solution.py:288
